TPU v7x, 32 devices: a whole 2x2x4 slice. The times are simulated.
32 devices in a mesh: dp: 4 (over z), ctx: 8 (over y, x, core).
Axes of the slice: x: 2, y: 2, z: 4, core: 2. Of those that a mesh axis runs over, the one named last changes fastest.
Arguments:
- queries: bfloat16 [8192, 1024], P(('dp', 'ctx')), may hold values from -27 to 27, as said below
- keys: bfloat16 [8192, 128], P(('dp', 'ctx')), may hold values from -4 to 4, as said below
- values: bfloat16 [8192, 128], P(('dp', 'ctx')), may hold values from -6 to 6
- grad_out: bfloat16 [8192, 1024], P(('dp', 'ctx')), may hold values from -6 to 6
- lengths: int32 [16], replicated, may hold values from 1 to 2048, 8192 in all
Outputs:
- attn_out: bfloat16 [8192, 1024], P(('dp', 'ctx'))
- grad_queries: bfloat16 [8192, 1024], P(('dp', 'ctx'))
- grad_keys: bfloat16 [8192, 128], P(('dp', 'ctx'))
- grad_values: bfloat16 [8192, 128], P(('dp', 'ctx'))
Inputs may be any that keep to these rules, and one draw needn't show every extreme that they name: `queries`: query entries lie in this range. `keys`: key entries lie in this range.
All inputs are finite; a program needn't handle non-finite values.
Results may differ from a plain program's by a relative error of at most 0.029.
Values may be sent and summed in bfloat16 or wider, within the bound.
No kernel may reach another device: no remote copies, remote signals or barrier semaphores. Data moves between devices by JAX's collectives and lax.ppermute only.
A program may use at most 192 MiB of HBM per device.

v0:
```python
import functools
import math

import jax
import jax.numpy as jnp
from jax import lax
from jax.experimental import pallas as pl
from jax.experimental.pallas import tpu as pltpu
from jax.sharding import PartitionSpec as P

HEADS = 8
HDIM = 128
NEG_FILL = -1e30
SCALE = float(HDIM) ** -0.5
EXP2_SCALE = SCALE * math.log2(math.e)

NT = (((1,), (1,)), ((), ()))
NN = (((1,), (0,)), ((), ()))


def dot(a, b, dims=NN):
    return lax.dot_general(a, b, dims, preferred_element_type=jnp.float32)


def route(n_dp, n_ctx, flip):
    pairs = []
    for d in range(n_dp):
        for c in range(n_ctx):
            run = d + int(c >= c ^ flip)
            if run < n_dp:
                pairs.append((d * n_ctx + c, run * n_ctx + (c ^ flip)))
    return pairs


def core_route(n_dp, n_ctx):
    return [(d * n_ctx + c, d * n_ctx + (c ^ 1)) for d in range(n_dp) for c in range(n_ctx)]


def attend(n_ctx, n_docs, group, index_ref, lengths_ref, q_ref, do_ref, own_kv, kv_z, kv_core, kv_direct, kv_passed,
           o_ref, dq_ref, g_own, g_z, g_core, g_direct, g_passed,
           kv, scores, probs, dscore, q_t, do_t, do_s, top, top_b, out_acc, corr, dq_acc, bias, grads, sems):
    rows = q_ref.shape[0]
    many = len(kv_direct)
    block = index_ref[0]
    ctx = lax.rem(block, n_ctx)
    base = block * rows

    copies = [pltpu.make_async_copy(own_kv, kv.at[n_ctx, :, pl.ds(0, 2 * HDIM)], sems.at[n_ctx]),
              pltpu.make_async_copy(kv_z, kv.at[0, :, pl.ds(0, 2 * HDIM)], sems.at[0]),
              pltpu.make_async_copy(kv_core, kv.at[1, :, pl.ds(0, 2 * HDIM)], sems.at[1])]
    for i in range(many):
        copies.append(pltpu.make_async_copy(kv_direct[i], kv.at[2 * i + 2, :, pl.ds(0, 2 * HDIM)], sems.at[2 * i + 2]))
        copies.append(pltpu.make_async_copy(kv_passed.at[i], kv.at[2 * i + 3, :, pl.ds(0, 2 * HDIM)], sems.at[2 * i + 3]))
    for copy in copies:
        copy.start()
    ones = jnp.ones((rows, HDIM), jnp.bfloat16)
    for slot in range(n_ctx + 1):
        kv[slot, :, 2 * HDIM:] = ones

    token = base + lax.broadcasted_iota(jnp.int32, (rows, rows), 0)
    start = jnp.zeros((rows, rows), jnp.int32)
    low = jnp.int32(0)
    end = jnp.int32(0)
    for i in range(n_docs):
        end = end + lengths_ref[i]
        start = jnp.where(token >= end, end, start)
        low = jnp.where(base >= end, end, low)
    before = lax.div(base - low + rows - 1, rows)
    first = start

    def slot_of(back):
        other = lax.rem(ctx - back + 2 * n_ctx, n_ctx)
        return jnp.where(back == 0, n_ctx, ctx ^ other)

    for h in range(HEADS):
        lanes = pl.ds(h * HDIM, HDIM)
        q_t[:, h * rows:(h + 1) * rows] = q_ref[:, lanes].astype(jnp.float32).T.astype(jnp.bfloat16)
    for copy in copies:
        copy.wait()

    bias[...] = first

    for g in range(HEADS // group):
        top[...] = jnp.full(top.shape, NEG_FILL, jnp.float32)

        @pl.loop(0, before + 1)
        def _(back):
            slot = slot_of(back)
            key = base - back * rows + lax.broadcasted_iota(jnp.int32, (rows, rows), 1)
            query = base + lax.broadcasted_iota(jnp.int32, (rows, rows), 0)
            off = jnp.where((key >= bias[...]) & (key <= query), 0.0, NEG_FILL)
            key_block = kv[slot, :, :HDIM]
            for i in range(group):
                h = g * group + i
                s = dot(q_ref[:, h * HDIM:(h + 1) * HDIM], key_block, NT) + off
                scores[back, i] = s
                top[i] = jnp.maximum(top[i], jnp.maximum(s[:, :HDIM], s[:, HDIM:]))

        for i in range(group):
            high = jnp.max(top[i], axis=1, keepdims=True) * EXP2_SCALE
            top_b[i] = jnp.broadcast_to(high, (rows, HDIM))
            out_acc[i] = jnp.zeros((rows, 2 * HDIM), jnp.float32)

        @pl.loop(0, before + 1)
        def _(back):
            slot = slot_of(back)
            value_block = kv[slot, :, HDIM:]
            for i in range(group):
                h = g * group + i
                high = top_b[i]
                s = scores[back, i]
                p = jnp.concatenate([jnp.exp2(s[:, :HDIM] * EXP2_SCALE - high), jnp.exp2(s[:, HDIM:] * EXP2_SCALE - high)], axis=1)
                p = p.astype(jnp.bfloat16)
                probs[back, h * rows:(h + 1) * rows, :] = p
                out_acc[i] += dot(p, value_block)

        for i in range(group):
            h = g * group + i
            lanes = pl.ds(h * HDIM, HDIM)
            acc = out_acc[i]
            inverse = 1.0 / acc[:, HDIM:]
            out = (acc[:, :HDIM] * inverse).astype(jnp.bfloat16)
            o_ref[:, lanes] = out
            grad = do_ref[:, lanes].astype(jnp.float32)
            correction = jnp.sum(grad * out.astype(jnp.float32), axis=1, keepdims=True)
            corr[h] = correction * inverse
            scaled = grad * inverse
            do_s[h] = scaled.astype(jnp.bfloat16)
            do_t[:, h * rows:(h + 1) * rows] = scaled.T.astype(jnp.bfloat16)
            dq_acc[h] = jnp.zeros((rows, HDIM), jnp.float32)

    @pl.loop(0, before + 1)
    def _(back):
        slot = slot_of(back)
        key_block = kv[slot, :, :HDIM]
        value_block = kv[slot, :, HDIM:2 * HDIM]
        for h in range(HEADS):
            d = dot(do_s[h], value_block, NT)
            c = corr[h]
            d = d - jnp.concatenate([c, c], axis=1)
            ds = (probs[back, h * rows:(h + 1) * rows, :].astype(jnp.float32) * d).astype(jnp.bfloat16)
            dscore[h * rows:(h + 1) * rows, :] = ds
            dq_acc[h] += dot(ds, key_block)
        dv_t = dot(do_t[...], probs[back])
        dk_t = dot(q_t[...], dscore[...])
        grads[slot, :, :HDIM] = dk_t.T
        grads[slot, :, HDIM:] = dv_t.T

    @pl.loop(before + 1, n_ctx + 1)
    def _(back):
        grads[slot_of(back)] = jnp.zeros((rows, 2 * HDIM), jnp.float32)

    for h in range(HEADS):
        lanes = pl.ds(h * HDIM, HDIM)
        dq_ref[:, lanes] = (dq_acc[h] * SCALE).astype(jnp.bfloat16)
    g_own[...] = grads[n_ctx]
    g_z[...] = grads[0].astype(jnp.bfloat16)
    g_core[...] = grads[1].astype(jnp.bfloat16)
    for i in range(many):
        g_direct[i] = grads[2 * i + 2].astype(jnp.bfloat16)
        g_passed[i] = grads[2 * i + 3].astype(jnp.bfloat16)


def shards(queries, keys, values, grad_out, lengths):
    rows = keys.shape[0]
    n_dp, n_ctx = lax.axis_size("dp"), lax.axis_size("ctx")
    n_docs = lengths.shape[0]
    axes = ("dp", "ctx")
    many = n_ctx // 2 - 1
    index = (lax.axis_index("dp") * n_ctx + lax.axis_index("ctx")).astype(jnp.int32).reshape(1)
    kv = jnp.concatenate([keys, values], axis=1)

    def permute(block, pairs):
        return lax.ppermute(block, axes, pairs)

    direct = [permute(kv, route(n_dp, n_ctx, 2 * i + 2)) for i in range(many)]
    core = permute(kv, route(n_dp, n_ctx, 1))
    above = permute(kv, route(n_dp, n_ctx, 0))
    passed = permute(jnp.stack(direct), core_route(n_dp, n_ctx))

    blocks = n_ctx + 1
    group = HEADS if blocks * HEADS * rows * rows * 6 <= 32 * 2**20 else HEADS // 2
    vmem = pl.BlockSpec(memory_space=pltpu.VMEM)
    smem = pl.BlockSpec(memory_space=pltpu.SMEM)
    hbm = pl.BlockSpec(memory_space=pl.ANY)
    f32, bf16 = jnp.float32, jnp.bfloat16
    shape = jax.ShapeDtypeStruct
    attn_out, grad_queries, g_own, g_z, g_core, g_direct, g_passed = pl.pallas_call(
        functools.partial(attend, n_ctx, n_docs, group),
        out_shape=(shape(queries.shape, bf16), shape(queries.shape, bf16), shape((rows, 2 * HDIM), f32),
                   shape((rows, 2 * HDIM), bf16), shape((rows, 2 * HDIM), bf16),
                   shape((many, rows, 2 * HDIM), bf16), shape((many, rows, 2 * HDIM), bf16)),
        in_specs=[smem, smem, vmem, vmem, hbm, hbm, hbm, [hbm] * many, hbm],
        out_specs=(vmem,) * 7,
        scratch_shapes=[
            pltpu.VMEM((blocks, rows, 3 * HDIM), bf16),
            pltpu.VMEM((blocks, group, rows, rows), f32),
            pltpu.VMEM((blocks, HEADS * rows, rows), bf16),
            pltpu.VMEM((HEADS * rows, rows), bf16),
            pltpu.VMEM((HDIM, HEADS * rows), bf16),
            pltpu.VMEM((HDIM, HEADS * rows), bf16),
            pltpu.VMEM((HEADS, rows, HDIM), bf16),
            pltpu.VMEM((group, rows, HDIM), f32),
            pltpu.VMEM((group, rows, HDIM), f32),
            pltpu.VMEM((group, rows, 2 * HDIM), f32),
            pltpu.VMEM((HEADS, rows, HDIM), f32),
            pltpu.VMEM((HEADS, rows, HDIM), f32),
            pltpu.VMEM((rows, rows), jnp.int32),
            pltpu.VMEM((blocks, rows, 2 * HDIM), f32),
            pltpu.SemaphoreType.DMA((blocks,)),
        ],
        compiler_params=pltpu.CompilerParams(vmem_limit_bytes=60 * 2**20),
        name="attend",
    )(index, lengths, queries, grad_out, kv, above, core, direct, passed)

    partner = permute(g_passed, core_route(n_dp, n_ctx))
    summed = g_direct.astype(f32) + partner.astype(f32)
    back = lambda pairs: [(b, a) for a, b in pairs]
    total = g_own
    for i in range(many):
        total = total + permute(summed[i].astype(bf16), back(route(n_dp, n_ctx, 2 * i + 2))).astype(f32)
    total = total + permute(g_core, back(route(n_dp, n_ctx, 1))).astype(f32)
    total = total + permute(g_z, back(route(n_dp, n_ctx, 0))).astype(f32)
    grad_keys = (total[:, :HDIM] * SCALE).astype(bf16)
    grad_values = total[:, HDIM:].astype(bf16)
    return (attn_out, grad_queries, grad_keys, grad_values)


def solution(mesh):
    tokens = P(("dp", "ctx"), None)
    return jax.shard_map(
        shards,
        mesh=mesh,
        in_specs=(tokens, tokens, tokens, tokens, P()),
        out_specs=(tokens, tokens, tokens, tokens),
        check_vma=False,
    )
```

profile of v0, /device:TPU:20, one launch (start us, length us, event | category | flops | bytes accessed | tf_op | source)
XLA Modules:
  0.0 72.2 jit_solution(12184436186645236059)
XLA Ops:
  0.6 0.0 copy-start.8
  0.6 0.9 %constant_dynamic-update-slice_fusion.1 = bf16[256,256]{1,0:T(8,128)(2,1)S(1)} fusion(bf16[256,128]{1,0:T(8,128)(2,1)} %param.6), kind=kLoop, calls=%fused_computation.10 | loop fusion | bytes 131072
  1.5 0.0 copy-done.8
  1.6 0.0 copy-start.4
  1.6 4.4 %collective-permute-start.4 = (bf16[256,256]{1,0:T(8,128)(2,1)S(1)}, bf16[256,256]{1,0:T(8,128)(2,1)S(1)}, u32[]{:S(2)}, u32[]{:S(2)}) collective-permute-start(bf16[256,256]{1,0:T(8,128)(2,1)S(1)} %constant_dynamic-update-slice_fusion.own_kv), channel_id=1, source_target_pairs={{0,6},{1,7},{2,4},{3,5},{4,10},{5,11},{6,8},{7,9},{8,14},{9,15},{1... | collective-permute-start | bytes 393224 | tf_op jit(solution)/shard_map/ppermute | solution.py:174
  5.9 3.4 %collective-permute-start.3 = (bf16[256,256]{1,0:T(8,128)(2,1)S(1)}, bf16[256,256]{1,0:T(8,128)(2,1)S(1)}, u32[]{:S(2)}, u32[]{:S(2)}) collective-permute-start(bf16[256,256]{1,0:T(8,128)(2,1)S(1)} %constant_dynamic-update-slice_fusion.own_kv), channel_id=1, source_target_pairs={{0,4},{1,5},{2,6},{3,7},{4,8},{5,9},{6,10},{7,11},{8,12},{9,13},{1... | collective-permute-start | bytes 393224 | tf_op jit(solution)/shard_map/ppermute | solution.py:174
  9.4 2.4 %collective-permute-start.2 = (bf16[256,256]{1,0:T(8,128)(2,1)S(1)}, bf16[256,256]{1,0:T(8,128)(2,1)S(1)}, u32[]{:S(2)}, u32[]{:S(2)}) collective-permute-start(bf16[256,256]{1,0:T(8,128)(2,1)S(1)} %constant_dynamic-update-slice_fusion.own_kv), channel_id=1, source_target_pairs={{0,2},{1,3},{2,8},{3,9},{4,6},{5,7},{6,12},{7,13},{8,10},{9,11},{1... | collective-permute-start | bytes 393224 | tf_op jit(solution)/shard_map/ppermute | solution.py:174
  11.8 0.0 collective-permute-done.4.kv_direct_2_
  11.8 0.0 copy-start
  11.8 1.0 %collective-permute-done.3.kv_direct_1_ = bf16[256,256]{1,0:T(8,128)(2,1)S(1)} collective-permute-done((bf16[256,256]{1,0:T(8,128)(2,1)S(1)}, bf16[256,256]{1,0:T(8,128)(2,1)S(1)}, u32[]{:S(2)}, u32[]{:S(2)}) %collective-permute-start.3) | collective-permute-done | bytes 131104 | tf_op jit(solution)/shard_map/ppermute | solution.py:174
  12.8 0.0 copy-start.1
  12.8 4.3 %collective-permute-done.2.kv_direct_0_ = bf16[256,256]{1,0:T(8,128)(2,1)S(1)} collective-permute-done((bf16[256,256]{1,0:T(8,128)(2,1)S(1)}, bf16[256,256]{1,0:T(8,128)(2,1)S(1)}, u32[]{:S(2)}, u32[]{:S(2)}) %collective-permute-start.2) | collective-permute-done | bytes 131104 | tf_op jit(solution)/shard_map/ppermute | solution.py:174
  17.1 0.0 copy-start.2
  17.2 0.0 copy-done
  17.2 0.0 copy-done.1
  17.2 0.6 copy-done.2
  17.8 0.0 collective-permute-start.5
  17.8 2.4 %collective-permute-start.1 = (bf16[256,256]{1,0:T(8,128)(2,1)S(1)}, bf16[256,256]{1,0:T(8,128)(2,1)S(1)}, u32[]{:S(2)}, u32[]{:S(2)}) collective-permute-start(bf16[256,256]{1,0:T(8,128)(2,1)S(1)} %constant_dynamic-update-slice_fusion.own_kv), channel_id=1, source_target_pairs={{0,1},{1,8},{2,3},{3,10},{4,5},{5,12},{6,7},{7,14},{8,9},{9,16},{1... | collective-permute-start | bytes 393224 | tf_op jit(solution)/shard_map/ppermute | solution.py:174
  20.2 0.0 copy-done.4
  20.2 2.4 %collective-permute-start = (bf16[256,256]{1,0:T(8,128)(2,1)S(1)}, bf16[256,256]{1,0:T(8,128)(2,1)S(1)}, u32[]{:S(2)}, u32[]{:S(2)}) collective-permute-start(bf16[256,256]{1,0:T(8,128)(2,1)S(1)} %constant_dynamic-update-slice_fusion.own_kv), channel_id=1, source_target_pairs={{0,8},{1,9},{2,10},{3,11},{4,12},{5,13},{6,14},{7,15},{8,16},{9,17... | collective-permute-start | bytes 393224 | tf_op jit(solution)/shard_map/ppermute | solution.py:174
  22.6 1.4 %collective-permute-done.1.kv_core = bf16[256,256]{1,0:T(8,128)(2,1)S(1)} collective-permute-done((bf16[256,256]{1,0:T(8,128)(2,1)S(1)}, bf16[256,256]{1,0:T(8,128)(2,1)S(1)}, u32[]{:S(2)}, u32[]{:S(2)}) %collective-permute-start.1) | collective-permute-done | bytes 131104 | tf_op jit(solution)/shard_map/ppermute | solution.py:174
  24.1 0.0 copy-start.6
  24.1 3.5 %collective-permute-done.kv_z = bf16[256,256]{1,0:T(8,128)(2,1)S(1)} collective-permute-done((bf16[256,256]{1,0:T(8,128)(2,1)S(1)}, bf16[256,256]{1,0:T(8,128)(2,1)S(1)}, u32[]{:S(2)}, u32[]{:S(2)}) %collective-permute-start) | collective-permute-done | bytes 131104 | tf_op jit(solution)/shard_map/ppermute | solution.py:174
  27.6 0.0 copy-start.7
  27.6 0.0 collective-permute-done.5.kv_passed
  27.6 0.0 copy-start.3
  27.6 0.0 copy-done.6
  27.6 0.7 copy-done.7
  28.3 0.1 copy-done.3
  28.4 18.9 %attend.1 = (bf16[256,1024]{1,0:T(8,128)(2,1)}, bf16[256,1024]{1,0:T(8,128)(2,1)}, f32[256,256]{1,0:T(8,128)}, bf16[256,256]{1,0:T(8,128)(2,1)}, bf16[256,256]{1...) custom-call(s32[1]{0:T(128)} %bitcast.index_ref, s32[16]{0:T(128)} %lengths_ref.1, ...), custom_call_target="tpu_custom_call" | custom-call | tf_op jit(solution)/shard_map/attend/pallas_call | solution.py:188
  47.3 1.5 %collective-permute-start.6 = (bf16[3,256,256]{2,1,0:T(8,128)(2,1)}, bf16[3,256,256]{2,1,0:T(8,128)(2,1)S(1)}, u32[]{:S(2)}, u32[]{:S(2)}) collective-permute-start(bf16[3,256,256]{2,1,0:T(8,128)(2,1)} %get-tuple-element.15), channel_id=1, source_target_pairs={{0,1},{1,0},{2,3},{3,2},{4,5},{5,4},{6,7},{7,6},{8,9},{9,8},{10,11... | collective-permute-start | bytes 1179656 | tf_op jit(solution)/shard_map/ppermute | solution.py:174
  48.9 1.9 %collective-permute-start.10 = (bf16[256,256]{1,0:T(8,128)(2,1)}, bf16[256,256]{1,0:T(8,128)(2,1)S(1)}, u32[]{:S(2)}, u32[]{:S(2)}) collective-permute-start(bf16[256,256]{1,0:T(8,128)(2,1)} %get-tuple-element.16), channel_id=1, source_target_pairs={{1,0},{8,1},{3,2},{10,3},{5,4},{12,5},{7,6},{14,7},{9,8},{16,9},{1... | collective-permute-start | bytes 393224 | tf_op jit(solution)/shard_map/ppermute | solution.py:174
  50.8 1.9 %collective-permute-start.11 = (bf16[256,256]{1,0:T(8,128)(2,1)}, bf16[256,256]{1,0:T(8,128)(2,1)S(1)}, u32[]{:S(2)}, u32[]{:S(2)}) collective-permute-start(bf16[256,256]{1,0:T(8,128)(2,1)} %get-tuple-element.17), channel_id=1, source_target_pairs={{8,0},{9,1},{10,2},{11,3},{12,4},{13,5},{14,6},{15,7},{16,8},{17,9... | collective-permute-start | bytes 393224 | tf_op jit(solution)/shard_map/ppermute | solution.py:174
  52.7 0.0 collective-permute-done.6
  52.7 1.1 %add_convert_fusion = bf16[3,256,256]{2,1,0:T(8,128)(2,1)S(1)} fusion(bf16[3,256,256]{2,1,0:T(8,128)(2,1)S(1)} %collective-permute-done.6, bf16[3,256,256]{2,1,0:T(8,128)(2,1)} %get-tuple-element.14), kind=kLoop, calls=%fused_computation | loop fusion | flops 786432 | bytes 1179648 | tf_op jit(solution)/shard_map/convert.3
  53.8 0.0 copy-start.5
  53.9 2.1 %collective-permute-start.7 = (bf16[256,256]{1,0:T(8,128)(2,1)S(1)}, bf16[256,256]{1,0:T(8,128)(2,1)S(1)}, u32[]{:S(2)}, u32[]{:S(2)}) collective-permute-start(bf16[256,256]{1,0:T(8,128)(2,1)S(1)} %get-tuple-element.18), channel_id=1, source_target_pairs={{2,0},{3,1},{8,2},{9,3},{6,4},{7,5},{12,6},{13,7},{10,8},{11,9},{1... | collective-permute-start | bytes 393224 | tf_op jit(solution)/shard_map/ppermute | solution.py:174
  55.9 1.9 %collective-permute-start.9 = (bf16[256,256]{1,0:T(8,128)(2,1)S(1)}, bf16[256,256]{1,0:T(8,128)(2,1)S(1)}, u32[]{:S(2)}, u32[]{:S(2)}) collective-permute-start(bf16[256,256]{1,0:T(8,128)(2,1)S(1)} %get-tuple-element.19), channel_id=1, source_target_pairs={{6,0},{7,1},{4,2},{5,3},{10,4},{11,5},{8,6},{9,7},{14,8},{15,9},{1... | collective-permute-start | bytes 393224 | tf_op jit(solution)/shard_map/ppermute | solution.py:174
  57.8 1.9 %collective-permute-start.8 = (bf16[256,256]{1,0:T(8,128)(2,1)S(1)}, bf16[256,256]{1,0:T(8,128)(2,1)S(1)}, u32[]{:S(2)}, u32[]{:S(2)}) collective-permute-start(bf16[256,256]{1,0:T(8,128)(2,1)S(1)} %get-tuple-element.20), channel_id=1, source_target_pairs={{4,0},{5,1},{6,2},{7,3},{8,4},{9,5},{10,6},{11,7},{12,8},{13,9},{1... | collective-permute-start | bytes 393224 | tf_op jit(solution)/shard_map/ppermute | solution.py:174
  59.8 0.0 collective-permute-done.10
  59.8 0.0 collective-permute-done.11
  59.8 4.4 %collective-permute-done.7 = bf16[256,256]{1,0:T(8,128)(2,1)S(1)} collective-permute-done((bf16[256,256]{1,0:T(8,128)(2,1)S(1)}, bf16[256,256]{1,0:T(8,128)(2,1)S(1)}, u32[]{:S(2)}, u32[]{:S(2)}) %collective-permute-start.7) | collective-permute-done | bytes 131104 | tf_op jit(solution)/shard_map/ppermute | solution.py:174
  64.2 1.3 %collective-permute-done.9 = bf16[256,256]{1,0:T(8,128)(2,1)S(1)} collective-permute-done((bf16[256,256]{1,0:T(8,128)(2,1)S(1)}, bf16[256,256]{1,0:T(8,128)(2,1)S(1)}, u32[]{:S(2)}, u32[]{:S(2)}) %collective-permute-start.9) | collective-permute-done | bytes 131104 | tf_op jit(solution)/shard_map/ppermute | solution.py:174
  65.5 5.3 %collective-permute-done.8 = bf16[256,256]{1,0:T(8,128)(2,1)S(1)} collective-permute-done((bf16[256,256]{1,0:T(8,128)(2,1)S(1)}, bf16[256,256]{1,0:T(8,128)(2,1)S(1)}, u32[]{:S(2)}, u32[]{:S(2)}) %collective-permute-start.8) | collective-permute-done | bytes 131104 | tf_op jit(solution)/shard_map/ppermute | solution.py:174
  70.8 0.0 copy-done.5
  70.8 0.1 convert_add_fusion
  70.9 0.6 slice.36
  71.5 0.6 fusion
  (3 shorter events, 0.1 us)
Async XLA Ops:
  0.6 0.9 %copy-start.8 = (bf16[256,128]{1,0:T(8,128)(2,1)S(1)}, bf16[256,128]{1,0:T(8,128)(2,1)}, u32[]{:S(2)}) copy-start(bf16[256,128]{1,0:T(8,128)(2,1)} %param.7) | copy-start | bytes 196612
  1.6 18.6 %copy-start.4 = (bf16[256,256]{1,0:T(8,128)(2,1)}, bf16[256,256]{1,0:T(8,128)(2,1)S(1)}, u32[]{:S(2)}) copy-start(bf16[256,256]{1,0:T(8,128)(2,1)S(1)} %constant_dynamic-update-slice_fusion.own_kv) | copy-start | bytes 393220
  1.6 10.3 %collective-permute-start.4 = (bf16[256,256]{1,0:T(8,128)(2,1)S(1)}, bf16[256,256]{1,0:T(8,128)(2,1)S(1)}, u32[]{:S(2)}, u32[]{:S(2)}) collective-permute-start(bf16[256,256]{1,0:T(8,128)(2,1)S(1)} %constant_dynamic-update-slice_fusion.own_kv), channel_id=1, source_target_pairs={{0,6},{1,7},{2,4},{3,5},{4,10},{5,11},{6,8},{7,9},{8,14},{9,15},{1... | collective-permute-start | bytes 393224 | tf_op jit(solution)/shard_map/ppermute | solution.py:174
  5.9 6.9 %collective-permute-start.3 = (bf16[256,256]{1,0:T(8,128)(2,1)S(1)}, bf16[256,256]{1,0:T(8,128)(2,1)S(1)}, u32[]{:S(2)}, u32[]{:S(2)}) collective-permute-start(bf16[256,256]{1,0:T(8,128)(2,1)S(1)} %constant_dynamic-update-slice_fusion.own_kv), channel_id=1, source_target_pairs={{0,4},{1,5},{2,6},{3,7},{4,8},{5,9},{6,10},{7,11},{8,12},{9,13},{1... | collective-permute-start | bytes 393224 | tf_op jit(solution)/shard_map/ppermute | solution.py:174
  9.4 7.8 %collective-permute-start.2 = (bf16[256,256]{1,0:T(8,128)(2,1)S(1)}, bf16[256,256]{1,0:T(8,128)(2,1)S(1)}, u32[]{:S(2)}, u32[]{:S(2)}) collective-permute-start(bf16[256,256]{1,0:T(8,128)(2,1)S(1)} %constant_dynamic-update-slice_fusion.own_kv), channel_id=1, source_target_pairs={{0,2},{1,3},{2,8},{3,9},{4,6},{5,7},{6,12},{7,13},{8,10},{9,11},{1... | collective-permute-start | bytes 393224 | tf_op jit(solution)/shard_map/ppermute | solution.py:174
  11.8 5.4 %copy-start = (bf16[256,256]{1,0:T(8,128)(2,1)}, bf16[256,256]{1,0:T(8,128)(2,1)S(1)}, u32[]{:S(2)}) copy-start(bf16[256,256]{1,0:T(8,128)(2,1)S(1)} %collective-permute-done.4.kv_direct_2_) | copy-start | bytes 393220
  12.8 4.4 %copy-start.1 = (bf16[256,256]{1,0:T(8,128)(2,1)}, bf16[256,256]{1,0:T(8,128)(2,1)S(1)}, u32[]{:S(2)}) copy-start(bf16[256,256]{1,0:T(8,128)(2,1)S(1)} %collective-permute-done.3.kv_direct_1_) | copy-start | bytes 393220
  17.1 0.6 copy-start.2
  17.8 9.8 %collective-permute-start.5 = (bf16[3,256,256]{2,1,0:T(8,128)(2,1)S(1)}, bf16[3,256,256]{2,1,0:T(8,128)(2,1)S(1)}, u32[]{:S(2)}, u32[]{:S(2)}) collective-permute-start(bf16[3,256,256]{2,1,0:T(8,128)(2,1)S(1)} %pad_maximum_fusion), channel_id=1, source_target_pairs={{0,1},{1,0},{2,3},{3,2},{4,5},{5,4},{6,7},{7,6},{8,9},{9,8},{10,11... | collective-permute-start | bytes 1179656 | tf_op jit(solution)/shard_map/ppermute | solution.py:174
  17.8 6.3 %collective-permute-start.1 = (bf16[256,256]{1,0:T(8,128)(2,1)S(1)}, bf16[256,256]{1,0:T(8,128)(2,1)S(1)}, u32[]{:S(2)}, u32[]{:S(2)}) collective-permute-start(bf16[256,256]{1,0:T(8,128)(2,1)S(1)} %constant_dynamic-update-slice_fusion.own_kv), channel_id=1, source_target_pairs={{0,1},{1,8},{2,3},{3,10},{4,5},{5,12},{6,7},{7,14},{8,9},{9,16},{1... | collective-permute-start | bytes 393224 | tf_op jit(solution)/shard_map/ppermute | solution.py:174
  20.2 7.4 %collective-permute-start = (bf16[256,256]{1,0:T(8,128)(2,1)S(1)}, bf16[256,256]{1,0:T(8,128)(2,1)S(1)}, u32[]{:S(2)}, u32[]{:S(2)}) collective-permute-start(bf16[256,256]{1,0:T(8,128)(2,1)S(1)} %constant_dynamic-update-slice_fusion.own_kv), channel_id=1, source_target_pairs={{0,8},{1,9},{2,10},{3,11},{4,12},{5,13},{6,14},{7,15},{8,16},{9,17... | collective-permute-start | bytes 393224 | tf_op jit(solution)/shard_map/ppermute | solution.py:174
  24.1 3.5 %copy-start.6 = (bf16[256,256]{1,0:T(8,128)(2,1)}, bf16[256,256]{1,0:T(8,128)(2,1)S(1)}, u32[]{:S(2)}) copy-start(bf16[256,256]{1,0:T(8,128)(2,1)S(1)} %collective-permute-done.1.kv_core) | copy-start | bytes 393220
  27.6 0.7 copy-start.7
  27.6 0.8 %copy-start.3 = (bf16[3,256,256]{2,1,0:T(8,128)(2,1)}, bf16[3,256,256]{2,1,0:T(8,128)(2,1)S(1)}, u32[]{:S(2)}) copy-start(bf16[3,256,256]{2,1,0:T(8,128)(2,1)S(1)} %collective-permute-done.5.kv_passed) | copy-start | bytes 1179652
  47.3 5.4 %collective-permute-start.6 = (bf16[3,256,256]{2,1,0:T(8,128)(2,1)}, bf16[3,256,256]{2,1,0:T(8,128)(2,1)S(1)}, u32[]{:S(2)}, u32[]{:S(2)}) collective-permute-start(bf16[3,256,256]{2,1,0:T(8,128)(2,1)} %get-tuple-element.15), channel_id=1, source_target_pairs={{0,1},{1,0},{2,3},{3,2},{4,5},{5,4},{6,7},{7,6},{8,9},{9,8},{10,11... | collective-permute-start | bytes 1179656 | tf_op jit(solution)/shard_map/ppermute | solution.py:174
  48.9 10.9 %collective-permute-start.10 = (bf16[256,256]{1,0:T(8,128)(2,1)}, bf16[256,256]{1,0:T(8,128)(2,1)S(1)}, u32[]{:S(2)}, u32[]{:S(2)}) collective-permute-start(bf16[256,256]{1,0:T(8,128)(2,1)} %get-tuple-element.16), channel_id=1, source_target_pairs={{1,0},{8,1},{3,2},{10,3},{5,4},{12,5},{7,6},{14,7},{9,8},{16,9},{1... | collective-permute-start | bytes 393224 | tf_op jit(solution)/shard_map/ppermute | solution.py:174
  50.8 9.0 %collective-permute-start.11 = (bf16[256,256]{1,0:T(8,128)(2,1)}, bf16[256,256]{1,0:T(8,128)(2,1)S(1)}, u32[]{:S(2)}, u32[]{:S(2)}) collective-permute-start(bf16[256,256]{1,0:T(8,128)(2,1)} %get-tuple-element.17), channel_id=1, source_target_pairs={{8,0},{9,1},{10,2},{11,3},{12,4},{13,5},{14,6},{15,7},{16,8},{17,9... | collective-permute-start | bytes 393224 | tf_op jit(solution)/shard_map/ppermute | solution.py:174
  53.8 17.0 %copy-start.5 = (f32[256,256]{1,0:T(8,128)S(1)}, f32[256,256]{1,0:T(8,128)}, u32[]{:S(2)}) copy-start(f32[256,256]{1,0:T(8,128)} %get-tuple-element.13) | copy-start | bytes 786436
  53.9 10.3 %collective-permute-start.7 = (bf16[256,256]{1,0:T(8,128)(2,1)S(1)}, bf16[256,256]{1,0:T(8,128)(2,1)S(1)}, u32[]{:S(2)}, u32[]{:S(2)}) collective-permute-start(bf16[256,256]{1,0:T(8,128)(2,1)S(1)} %get-tuple-element.18), channel_id=1, source_target_pairs={{2,0},{3,1},{8,2},{9,3},{6,4},{7,5},{12,6},{13,7},{10,8},{11,9},{1... | collective-permute-start | bytes 393224 | tf_op jit(solution)/shard_map/ppermute | solution.py:174
  55.9 9.6 %collective-permute-start.9 = (bf16[256,256]{1,0:T(8,128)(2,1)S(1)}, bf16[256,256]{1,0:T(8,128)(2,1)S(1)}, u32[]{:S(2)}, u32[]{:S(2)}) collective-permute-start(bf16[256,256]{1,0:T(8,128)(2,1)S(1)} %get-tuple-element.19), channel_id=1, source_target_pairs={{6,0},{7,1},{4,2},{5,3},{10,4},{11,5},{8,6},{9,7},{14,8},{15,9},{1... | collective-permute-start | bytes 393224 | tf_op jit(solution)/shard_map/ppermute | solution.py:174
  57.8 13.0 %collective-permute-start.8 = (bf16[256,256]{1,0:T(8,128)(2,1)S(1)}, bf16[256,256]{1,0:T(8,128)(2,1)S(1)}, u32[]{:S(2)}, u32[]{:S(2)}) collective-permute-start(bf16[256,256]{1,0:T(8,128)(2,1)S(1)} %get-tuple-element.20), channel_id=1, source_target_pairs={{4,0},{5,1},{6,2},{7,3},{8,4},{9,5},{10,6},{11,7},{12,8},{13,9},{1... | collective-permute-start | bytes 393224 | tf_op jit(solution)/shard_map/ppermute | solution.py:174
where the time goes:
time: 71 us; the launch traced here: 72.2 us
  starting transfers between devices  26.3 us (37%)
  waiting for transfers between devices  21.3 us (30%)
  Pallas kernels  18.9 us (27%)
  local copies, waits for them, and re-layouts  2.96 us (4%)
  other arithmetic  1.88 us (3%)
  between operations  0.86 us (1%)
    ppermute x12, starting transfers between devices, permute(): return lax.ppermute(block, axes, pairs)  26.3 us
    ppermute x12, waiting for transfers between devices, permute(): return lax.ppermute(block, axes, pairs)  21.3 us
    pallas_call x1, Pallas kernels, shards(): pl.pallas_call(functools.partial(attend, n_ctx, n_docs, group), out_shape...  18.9 us
    unnamed x19, local copies, waits for them, and re-layouts  2.27 us
  transfers between devices with their start and end apart: 12, of which 7 were waited for; matrix products, arithmetic and copies ran while one was open for 2% of the time, Pallas kernels for 0%

commit v1 on v0

--- a/solution.py
+++ b/solution.py
@@ -22,37 +22,29 @@
     return lax.dot_general(a, b, dims, preferred_element_type=jnp.float32)
 
 
-def route(n_dp, n_ctx, flip):
-    pairs = []
-    for d in range(n_dp):
-        for c in range(n_ctx):
-            run = d + int(c >= c ^ flip)
-            if run < n_dp:
-                pairs.append((d * n_ctx + c, run * n_ctx + (c ^ flip)))
-    return pairs
-
-
-def core_route(n_dp, n_ctx):
-    return [(d * n_ctx + c, d * n_ctx + (c ^ 1)) for d in range(n_dp) for c in range(n_ctx)]
-
-
-def attend(n_ctx, n_docs, group, index_ref, lengths_ref, q_ref, do_ref, own_kv, kv_z, kv_core, kv_direct, kv_passed,
-           o_ref, dq_ref, g_own, g_z, g_core, g_direct, g_passed,
-           kv, scores, probs, dscore, q_t, do_t, do_s, top, top_b, out_acc, corr, dq_acc, bias, grads, sems):
+def run_route(n_dp, n_ctx):
+    return [(d * n_ctx + c, (d + 1) * n_ctx + c) for d in range(n_dp - 1) for c in range(n_ctx)]
+
+
+def flip_route(n_dp, n_ctx, flip):
+    return [(d * n_ctx + c, d * n_ctx + (c ^ flip)) for d in range(n_dp) for c in range(n_ctx)]
+
+
+def attend(n_ctx, n_docs, group, index_ref, lengths_ref, q_ref, do_ref, own_kv, kv_prev, kv_direct, kv_passed,
+           o_ref, dq_ref, g_own, g_prev, g_direct, g_passed,
+           kv, scores, probs, dscore, q_t, do_t, do_s, top, top_b, out_acc, corr, dq_acc, bias, grads):
     rows = q_ref.shape[0]
-    many = len(kv_direct)
+    many = kv_passed.shape[0]
     block = index_ref[0]
     ctx = lax.rem(block, n_ctx)
     base = block * rows
 
-    copies = [pltpu.make_async_copy(own_kv, kv.at[n_ctx, :, pl.ds(0, 2 * HDIM)], sems.at[n_ctx]),
-              pltpu.make_async_copy(kv_z, kv.at[0, :, pl.ds(0, 2 * HDIM)], sems.at[0]),
-              pltpu.make_async_copy(kv_core, kv.at[1, :, pl.ds(0, 2 * HDIM)], sems.at[1])]
+    kv[n_ctx, :, :2 * HDIM] = own_kv[...]
+    kv[0, :, :2 * HDIM] = kv_prev[...]
     for i in range(many):
-        copies.append(pltpu.make_async_copy(kv_direct[i], kv.at[2 * i + 2, :, pl.ds(0, 2 * HDIM)], sems.at[2 * i + 2]))
-        copies.append(pltpu.make_async_copy(kv_passed.at[i], kv.at[2 * i + 3, :, pl.ds(0, 2 * HDIM)], sems.at[2 * i + 3]))
-    for copy in copies:
-        copy.start()
+        kv[2 * i + 1, :, :2 * HDIM] = kv_passed[i]
+        if i > 0:
+            kv[2 * i, :, :2 * HDIM] = kv_direct[i - 1][...]
     ones = jnp.ones((rows, HDIM), jnp.bfloat16)
     for slot in range(n_ctx + 1):
         kv[slot, :, 2 * HDIM:] = ones
@@ -75,9 +67,6 @@
     for h in range(HEADS):
         lanes = pl.ds(h * HDIM, HDIM)
         q_t[:, h * rows:(h + 1) * rows] = q_ref[:, lanes].astype(jnp.float32).T.astype(jnp.bfloat16)
-    for copy in copies:
-        copy.wait()
-
     bias[...] = first
 
     for g in range(HEADS // group):
@@ -154,11 +143,11 @@
         lanes = pl.ds(h * HDIM, HDIM)
         dq_ref[:, lanes] = (dq_acc[h] * SCALE).astype(jnp.bfloat16)
     g_own[...] = grads[n_ctx]
-    g_z[...] = grads[0].astype(jnp.bfloat16)
-    g_core[...] = grads[1].astype(jnp.bfloat16)
+    g_prev[...] = grads[0]
     for i in range(many):
-        g_direct[i] = grads[2 * i + 2].astype(jnp.bfloat16)
-        g_passed[i] = grads[2 * i + 3].astype(jnp.bfloat16)
+        g_passed[i] = grads[2 * i + 1].astype(jnp.bfloat16)
+        if i > 0:
+            g_direct[i - 1] = grads[2 * i].astype(jnp.bfloat16)
 
 
 def shards(queries, keys, values, grad_out, lengths):
@@ -166,32 +155,35 @@
     n_dp, n_ctx = lax.axis_size("dp"), lax.axis_size("ctx")
     n_docs = lengths.shape[0]
     axes = ("dp", "ctx")
-    many = n_ctx // 2 - 1
-    index = (lax.axis_index("dp") * n_ctx + lax.axis_index("ctx")).astype(jnp.int32).reshape(1)
+    many = n_ctx // 2
+    ctx = lax.axis_index("ctx")
+    index = (lax.axis_index("dp") * n_ctx + ctx).astype(jnp.int32).reshape(1)
     kv = jnp.concatenate([keys, values], axis=1)
 
-    def permute(block, pairs):
-        return lax.ppermute(block, axes, pairs)
-
-    direct = [permute(kv, route(n_dp, n_ctx, 2 * i + 2)) for i in range(many)]
-    core = permute(kv, route(n_dp, n_ctx, 1))
-    above = permute(kv, route(n_dp, n_ctx, 0))
-    passed = permute(jnp.stack(direct), core_route(n_dp, n_ctx))
+    def swap(block, flip):
+        return lax.ppermute(block, axes, flip_route(n_dp, n_ctx, flip))
+
+    def later(flip):
+        return ctx < ctx ^ flip
+
+    prev = lax.ppermute(kv, axes, run_route(n_dp, n_ctx))
+    sent = [jnp.where(later(max(2 * i, 1)), kv, prev) for i in range(many)]
+    direct = [swap(sent[i], 2 * i) for i in range(1, many)]
+    passed = swap(jnp.stack([sent[0]] + direct), 1)
 
     blocks = n_ctx + 1
     group = HEADS if blocks * HEADS * rows * rows * 6 <= 32 * 2**20 else HEADS // 2
     vmem = pl.BlockSpec(memory_space=pltpu.VMEM)
     smem = pl.BlockSpec(memory_space=pltpu.SMEM)
-    hbm = pl.BlockSpec(memory_space=pl.ANY)
     f32, bf16 = jnp.float32, jnp.bfloat16
     shape = jax.ShapeDtypeStruct
-    attn_out, grad_queries, g_own, g_z, g_core, g_direct, g_passed = pl.pallas_call(
+    attn_out, grad_queries, g_own, g_prev, g_direct, g_passed = pl.pallas_call(
         functools.partial(attend, n_ctx, n_docs, group),
         out_shape=(shape(queries.shape, bf16), shape(queries.shape, bf16), shape((rows, 2 * HDIM), f32),
-                   shape((rows, 2 * HDIM), bf16), shape((rows, 2 * HDIM), bf16),
-                   shape((many, rows, 2 * HDIM), bf16), shape((many, rows, 2 * HDIM), bf16)),
-        in_specs=[smem, smem, vmem, vmem, hbm, hbm, hbm, [hbm] * many, hbm],
-        out_specs=(vmem,) * 7,
+                   shape((rows, 2 * HDIM), f32), shape((many - 1, rows, 2 * HDIM), bf16),
+                   shape((many, rows, 2 * HDIM), bf16)),
+        in_specs=[smem, smem, vmem, vmem, vmem, vmem, [vmem] * (many - 1), vmem],
+        out_specs=(vmem,) * 6,
         scratch_shapes=[
             pltpu.VMEM((blocks, rows, 3 * HDIM), bf16),
             pltpu.VMEM((blocks, group, rows, rows), f32),
@@ -207,20 +199,22 @@
             pltpu.VMEM((HEADS, rows, HDIM), f32),
             pltpu.VMEM((rows, rows), jnp.int32),
             pltpu.VMEM((blocks, rows, 2 * HDIM), f32),
-            pltpu.SemaphoreType.DMA((blocks,)),
         ],
         compiler_params=pltpu.CompilerParams(vmem_limit_bytes=60 * 2**20),
         name="attend",
-    )(index, lengths, queries, grad_out, kv, above, core, direct, passed)
-
-    partner = permute(g_passed, core_route(n_dp, n_ctx))
-    summed = g_direct.astype(f32) + partner.astype(f32)
-    back = lambda pairs: [(b, a) for a, b in pairs]
-    total = g_own
+    )(index, lengths, queries, grad_out, kv, prev, direct, passed)
+
+    partner = swap(g_passed, 1).astype(f32)
+    own_total, prev_total = g_own, g_prev
     for i in range(many):
-        total = total + permute(summed[i].astype(bf16), back(route(n_dp, n_ctx, 2 * i + 2))).astype(f32)
-    total = total + permute(g_core, back(route(n_dp, n_ctx, 1))).astype(f32)
-    total = total + permute(g_z, back(route(n_dp, n_ctx, 0))).astype(f32)
+        term = partner[0]
+        if i > 0:
+            term = swap((g_direct[i - 1].astype(f32) + partner[i]).astype(bf16), 2 * i).astype(f32)
+        ours = later(max(2 * i, 1))
+        own_total = own_total + jnp.where(ours, term, 0.0)
+        prev_total = prev_total + jnp.where(ours, 0.0, term)
+    back = [(b, a) for a, b in run_route(n_dp, n_ctx)]
+    total = own_total + lax.ppermute(prev_total.astype(bf16), axes, back).astype(f32)
     grad_keys = (total[:, :HDIM] * SCALE).astype(bf16)
     grad_values = total[:, HDIM:].astype(bf16)
     return (attn_out, grad_queries, grad_keys, grad_values)

time: 71 us -> 66.1 us (0.931)
  the two profiles are of different devices: /device:TPU:20 before, /device:TPU:0 now
where the time goes in v1:
time: 66.1 us; the launch traced here: 66.9 us
  waiting for transfers between devices  35.2 us (53%)
  starting transfers between devices  19 us (29%)
  Pallas kernels  7.19 us (11%)
  local copies, waits for them, and re-layouts  3.54 us (5%)
  other arithmetic  1.16 us (2%)
  between operations  0.78 us (1%)
    ppermute x1, waiting for transfers between devices, shards(): lax.ppermute(prev_total.astype(bf16), axes, back).astype(f32)  18 us
    ppermute x8, waiting for transfers between devices, swap(): return lax.ppermute(block, axes, flip_route(n_dp, n_ctx, flip))  14.5 us
    ppermute x8, starting transfers between devices, swap(): return lax.ppermute(block, axes, flip_route(n_dp, n_ctx, flip))  12.8 us
    pallas_call x1, Pallas kernels, shards(): pl.pallas_call(functools.partial(attend, n_ctx, n_docs, group), out_shape...  7.19 us
    ppermute x1, starting transfers between devices, shards(): prev = lax.ppermute(kv, axes, run_route(n_dp, n_ctx))  4.94 us
    unnamed x21, local copies, waits for them, and re-layouts  2.88 us
    ppermute x1, waiting for transfers between devices, shards(): prev = lax.ppermute(kv, axes, run_route(n_dp, n_ctx))  2.71 us
  transfers between devices with their start and end apart: 10, of which 9 were waited for; matrix products, arithmetic and copies ran while one was open for 0% of the time, Pallas kernels for 0%

profile of v1, /device:TPU:0, one launch (start us, length us, event | category | flops | bytes accessed | tf_op | source)
XLA Modules:
  0.0 66.9 jit_solution(14922889010971504645)
XLA Ops:
  0.6 0.0 copy-start.9
  0.6 0.9 %constant_dynamic-update-slice_fusion.1 = bf16[256,256]{1,0:T(8,128)(2,1)S(1)} fusion(bf16[256,128]{1,0:T(8,128)(2,1)} %param.6), kind=kLoop, calls=%fused_computation.34 | loop fusion | bytes 131072
  1.5 0.0 copy-done.9
  1.6 0.0 copy-start
  1.6 4.9 %collective-permute-start = (bf16[256,256]{1,0:T(8,128)(2,1)S(1)}, bf16[256,256]{1,0:T(8,128)(2,1)S(1)}, u32[]{:S(2)}, u32[]{:S(2)}) collective-permute-start(bf16[256,256]{1,0:T(8,128)(2,1)S(1)} %constant_dynamic-update-slice_fusion.own_kv), channel_id=1, source_target_pairs={{0,8},{1,9},{2,10},{3,11},{4,12},{5,13},{6,14},{7,15},{8,16},{9,17... | collective-permute-start | bytes 393224 | tf_op jit(solution)/shard_map/ppermute | solution.py:169
  6.5 2.7 %collective-permute-done.kv_prev = bf16[256,256]{1,0:T(8,128)(2,1)S(1)} collective-permute-done((bf16[256,256]{1,0:T(8,128)(2,1)S(1)}, bf16[256,256]{1,0:T(8,128)(2,1)S(1)}, u32[]{:S(2)}, u32[]{:S(2)}) %collective-permute-start) | collective-permute-done | bytes 131104 | tf_op jit(solution)/shard_map/ppermute | solution.py:169
  9.2 0.0 copy-start.1
  9.3 0.0 copy-done
  9.3 0.6 copy-done.1
  9.9 2.4 %collective-permute-start.3 = (bf16[256,256]{1,0:T(8,128)(2,1)S(1)}, bf16[256,256]{1,0:T(8,128)(2,1)S(1)}, u32[]{:S(2)}, u32[]{:S(2)}) collective-permute-start(bf16[256,256]{1,0:T(8,128)(2,1)S(1)} %get-tuple-element.20), channel_id=1, source_target_pairs={{0,6},{1,7},{2,4},{3,5},{4,2},{5,3},{6,0},{7,1},{8,14},{9,15},{10,... | collective-permute-start | bytes 393224 | tf_op jit(solution)/shard_map/ppermute | solution.py:164
  12.3 0.5 collective-permute-start.2
  12.9 0.5 collective-permute-start.1
  13.4 3.4 %collective-permute-done.3.kv_direct_2_ = bf16[256,256]{1,0:T(8,128)(2,1)S(1)} collective-permute-done((bf16[256,256]{1,0:T(8,128)(2,1)S(1)}, bf16[256,256]{1,0:T(8,128)(2,1)S(1)}, u32[]{:S(2)}, u32[]{:S(2)}) %collective-permute-start.3) | collective-permute-done | bytes 131104 | tf_op jit(solution)/shard_map/ppermute | solution.py:164
  16.8 0.0 copy-start.3
  16.8 1.2 %collective-permute-done.2.kv_direct_1_ = bf16[256,256]{1,0:T(8,128)(2,1)S(1)} collective-permute-done((bf16[256,256]{1,0:T(8,128)(2,1)S(1)}, bf16[256,256]{1,0:T(8,128)(2,1)S(1)}, u32[]{:S(2)}, u32[]{:S(2)}) %collective-permute-start.2) | collective-permute-done | bytes 131104 | tf_op jit(solution)/shard_map/ppermute | solution.py:164
  18.0 0.0 copy-start.4
  18.0 0.1 collective-permute-done.1.kv_direct_0_
  18.1 0.0 copy-start.5
  18.1 0.1 pad_maximum_fusion
  18.1 0.0 copy-done.3
  18.2 0.5 copy-done.4
  18.6 0.1 copy-done.5
  18.7 0.0 collective-permute-start.4
  18.7 1.9 %collective-permute-done.4.kv_passed = bf16[4,256,256]{2,1,0:T(8,128)(2,1)S(1)} collective-permute-done((bf16[4,256,256]{2,1,0:T(8,128)(2,1)S(1)}, bf16[4,256,256]{2,1,0:T(8,128)(2,1)S(1)}, u32[]{:S(2)}, u32[]{:S(2)}) %collective-permute-start.4) | collective-permute-done | bytes 524320 | tf_op jit(solution)/shard_map/ppermute | solution.py:164
  20.6 0.0 copy-start.2
  20.6 0.8 %copy-done.2 = bf16[4,256,256]{2,1,0:T(8,128)(2,1)} copy-done((bf16[4,256,256]{2,1,0:T(8,128)(2,1)}, bf16[4,256,256]{2,1,0:T(8,128)(2,1)S(1)}, u32[]{:S(2)}) %copy-start.2) | copy-done | bytes 524312
  21.4 7.2 %attend.1 = (bf16[256,1024]{1,0:T(8,128)(2,1)}, bf16[256,1024]{1,0:T(8,128)(2,1)}, f32[256,256]{1,0:T(8,128)}, f32[256,256]{1,0:T(8,128)}, bf16[3,256,256]{2,1,0:T(8,128)(2,1)}, /*index=5*/bf16[4,256,256]{2,1,0:T(8,128)(2,1)}) custom-call(s32[1]{0:T(128)} %bitcast.index_ref, s32[16]{0:T(128)} %lengths_ref.1, bf16[256,1024]{1,0:T(8,128)(2,1)} %q_ref.1, ...), custom_call_target="tpu_custom_call" | custom-call | tf_op jit(solution)/shard_map/attend/pallas_call | solution.py:180
  28.6 0.0 copy-start.6
  28.6 2.4 %collective-permute-start.5 = (bf16[4,256,256]{2,1,0:T(8,128)(2,1)}, bf16[4,256,256]{2,1,0:T(8,128)(2,1)S(1)}, u32[]{:S(2)}, u32[]{:S(2)}) collective-permute-start(bf16[4,256,256]{2,1,0:T(8,128)(2,1)} %get-tuple-element.13), channel_id=1, source_target_pairs={{0,1},{1,0},{2,3},{3,2},{4,5},{5,4},{6,7},{7,6},{8,9},{9,8},{10,11... | collective-permute-start | bytes 1572872 | tf_op jit(solution)/shard_map/ppermute | solution.py:164
  31.0 1.7 %collective-permute-done.5 = bf16[4,256,256]{2,1,0:T(8,128)(2,1)S(1)} collective-permute-done((bf16[4,256,256]{2,1,0:T(8,128)(2,1)}, bf16[4,256,256]{2,1,0:T(8,128)(2,1)S(1)}, u32[]{:S(2)}, u32[]{:S(2)}) %collective-permute-start.5) | collective-permute-done | bytes 524320 | tf_op jit(solution)/shard_map/ppermute | solution.py:164
  32.8 0.1 convert_element_type.52
  32.9 0.0 copy-done.6
  32.9 0.0 copy-start.8
  32.9 0.1 fusion.13
  33.0 6.3 %collective-permute-start.8 = (bf16[256,256]{1,0:T(8,128)(2,1)S(1)}, bf16[256,256]{1,0:T(8,128)(2,1)S(1)}, u32[]{:S(2)}, u32[]{:S(2)}) collective-permute-start(bf16[256,256]{1,0:T(8,128)(2,1)S(1)} %get-tuple-element.16), channel_id=1, source_target_pairs={{0,6},{1,7},{2,4},{3,5},{4,2},{5,3},{6,0},{7,1},{8,14},{9,15},{10,... | collective-permute-start | bytes 393224 | tf_op jit(solution)/shard_map/ppermute | solution.py:164
  39.3 0.0 collective-permute-start.7
  39.3 0.6 collective-permute-start.6
  39.9 3.5 %collective-permute-done.8 = bf16[256,256]{1,0:T(8,128)(2,1)S(1)} collective-permute-done((bf16[256,256]{1,0:T(8,128)(2,1)S(1)}, bf16[256,256]{1,0:T(8,128)(2,1)S(1)}, u32[]{:S(2)}, u32[]{:S(2)}) %collective-permute-start.8) | collective-permute-done | bytes 131104 | tf_op jit(solution)/shard_map/ppermute | solution.py:164
  43.4 2.7 %collective-permute-done.7 = bf16[256,256]{1,0:T(8,128)(2,1)S(1)} collective-permute-done((bf16[256,256]{1,0:T(8,128)(2,1)S(1)}, bf16[256,256]{1,0:T(8,128)(2,1)S(1)}, u32[]{:S(2)}, u32[]{:S(2)}) %collective-permute-start.7) | collective-permute-done | bytes 131104 | tf_op jit(solution)/shard_map/ppermute | solution.py:164
  46.1 0.0 collective-permute-done.6
  46.1 0.0 copy-done.8
  46.1 0.0 copy-start.7
  46.1 0.1 fusion.7
  46.2 1.3 %collective-permute-start.9 = (bf16[256,256]{1,0:T(8,128)(2,1)S(1)}, bf16[256,256]{1,0:T(8,128)(2,1)S(1)}, u32[]{:S(2)}, u32[]{:S(2)}) collective-permute-start(bf16[256,256]{1,0:T(8,128)(2,1)S(1)} %fusion.7), channel_id=1, source_target_pairs={{8,0},{9,1},{10,2},{11,3},{12,4},{13,5},{14,6},{15,7},{16,8},{17,9... | collective-permute-start | bytes 393224 | tf_op jit(solution)/shard_map/ppermute | solution.py:217
  47.5 18.0 %collective-permute-done.9 = bf16[256,256]{1,0:T(8,128)(2,1)S(1)} collective-permute-done((bf16[256,256]{1,0:T(8,128)(2,1)S(1)}, bf16[256,256]{1,0:T(8,128)(2,1)S(1)}, u32[]{:S(2)}, u32[]{:S(2)}) %collective-permute-start.9) | collective-permute-done | bytes 131104 | tf_op jit(solution)/shard_map/ppermute | solution.py:217
  65.5 0.0 copy-done.7
  65.5 0.1 fusion.3
  65.6 0.6 slice.67
  66.3 0.6 fusion.14
  (2 shorter events, 0.1 us)
Async XLA Ops:
  0.6 0.9 %copy-start.9 = (bf16[256,128]{1,0:T(8,128)(2,1)S(1)}, bf16[256,128]{1,0:T(8,128)(2,1)}, u32[]{:S(2)}) copy-start(bf16[256,128]{1,0:T(8,128)(2,1)} %param.7) | copy-start | bytes 196612
  1.6 7.7 %copy-start = (bf16[256,256]{1,0:T(8,128)(2,1)}, bf16[256,256]{1,0:T(8,128)(2,1)S(1)}, u32[]{:S(2)}) copy-start(bf16[256,256]{1,0:T(8,128)(2,1)S(1)} %constant_dynamic-update-slice_fusion.own_kv) | copy-start | bytes 393220
  1.6 7.7 %collective-permute-start = (bf16[256,256]{1,0:T(8,128)(2,1)S(1)}, bf16[256,256]{1,0:T(8,128)(2,1)S(1)}, u32[]{:S(2)}, u32[]{:S(2)}) collective-permute-start(bf16[256,256]{1,0:T(8,128)(2,1)S(1)} %constant_dynamic-update-slice_fusion.own_kv), channel_id=1, source_target_pairs={{0,8},{1,9},{2,10},{3,11},{4,12},{5,13},{6,14},{7,15},{8,16},{9,17... | collective-permute-start | bytes 393224 | tf_op jit(solution)/shard_map/ppermute | solution.py:169
  9.2 0.7 copy-start.1
  9.9 6.9 %collective-permute-start.3 = (bf16[256,256]{1,0:T(8,128)(2,1)S(1)}, bf16[256,256]{1,0:T(8,128)(2,1)S(1)}, u32[]{:S(2)}, u32[]{:S(2)}) collective-permute-start(bf16[256,256]{1,0:T(8,128)(2,1)S(1)} %get-tuple-element.20), channel_id=1, source_target_pairs={{0,6},{1,7},{2,4},{3,5},{4,2},{5,3},{6,0},{7,1},{8,14},{9,15},{10,... | collective-permute-start | bytes 393224 | tf_op jit(solution)/shard_map/ppermute | solution.py:164
  12.3 5.6 %collective-permute-start.2 = (bf16[256,256]{1,0:T(8,128)(2,1)S(1)}, bf16[256,256]{1,0:T(8,128)(2,1)S(1)}, u32[]{:S(2)}, u32[]{:S(2)}) collective-permute-start(bf16[256,256]{1,0:T(8,128)(2,1)S(1)} %get-tuple-element.21), channel_id=1, source_target_pairs={{0,4},{1,5},{2,6},{3,7},{4,0},{5,1},{6,2},{7,3},{8,12},{9,13},{10,... | collective-permute-start | bytes 393224 | tf_op jit(solution)/shard_map/ppermute | solution.py:164
  12.9 5.2 %collective-permute-start.1 = (bf16[256,256]{1,0:T(8,128)(2,1)S(1)}, bf16[256,256]{1,0:T(8,128)(2,1)S(1)}, u32[]{:S(2)}, u32[]{:S(2)}) collective-permute-start(bf16[256,256]{1,0:T(8,128)(2,1)S(1)} %get-tuple-element.22), channel_id=1, source_target_pairs={{0,2},{1,3},{2,0},{3,1},{4,6},{5,7},{6,4},{7,5},{8,10},{9,11},{10,... | collective-permute-start | bytes 393224 | tf_op jit(solution)/shard_map/ppermute | solution.py:164
  16.8 1.3 %copy-start.3 = (bf16[256,256]{1,0:T(8,128)(2,1)}, bf16[256,256]{1,0:T(8,128)(2,1)S(1)}, u32[]{:S(2)}) copy-start(bf16[256,256]{1,0:T(8,128)(2,1)S(1)} %collective-permute-done.3.kv_direct_2_) | copy-start | bytes 393220
  18.0 0.7 copy-start.4
  18.1 0.6 copy-start.5
  18.7 1.9 %collective-permute-start.4 = (bf16[4,256,256]{2,1,0:T(8,128)(2,1)S(1)}, bf16[4,256,256]{2,1,0:T(8,128)(2,1)S(1)}, u32[]{:S(2)}, u32[]{:S(2)}) collective-permute-start(bf16[4,256,256]{2,1,0:T(8,128)(2,1)S(1)} %pad_maximum_fusion), channel_id=1, source_target_pairs={{0,1},{1,0},{2,3},{3,2},{4,5},{5,4},{6,7},{7,6},{8,9},{9,8},{10,11... | collective-permute-start | bytes 1572872 | tf_op jit(solution)/shard_map/ppermute | solution.py:164
  20.6 0.8 %copy-start.2 = (bf16[4,256,256]{2,1,0:T(8,128)(2,1)}, bf16[4,256,256]{2,1,0:T(8,128)(2,1)S(1)}, u32[]{:S(2)}) copy-start(bf16[4,256,256]{2,1,0:T(8,128)(2,1)S(1)} %collective-permute-done.4.kv_passed) | copy-start | bytes 1572868
  28.6 4.3 %copy-start.6 = (bf16[3,256,256]{2,1,0:T(8,128)(2,1)S(1)}, bf16[3,256,256]{2,1,0:T(8,128)(2,1)}, u32[]{:S(2)}) copy-start(bf16[3,256,256]{2,1,0:T(8,128)(2,1)} %get-tuple-element.14) | copy-start | bytes 1179652
  28.6 4.2 %collective-permute-start.5 = (bf16[4,256,256]{2,1,0:T(8,128)(2,1)}, bf16[4,256,256]{2,1,0:T(8,128)(2,1)S(1)}, u32[]{:S(2)}, u32[]{:S(2)}) collective-permute-start(bf16[4,256,256]{2,1,0:T(8,128)(2,1)} %get-tuple-element.13), channel_id=1, source_target_pairs={{0,1},{1,0},{2,3},{3,2},{4,5},{5,4},{6,7},{7,6},{8,9},{9,8},{10,11... | collective-permute-start | bytes 1572872 | tf_op jit(solution)/shard_map/ppermute | solution.py:164
  32.9 13.2 %copy-start.8 = (f32[256,256]{1,0:T(8,128)S(1)}, f32[256,256]{1,0:T(8,128)}, u32[]{:S(2)}) copy-start(f32[256,256]{1,0:T(8,128)} %get-tuple-element.15) | copy-start | bytes 786436
  33.0 10.4 %collective-permute-start.8 = (bf16[256,256]{1,0:T(8,128)(2,1)S(1)}, bf16[256,256]{1,0:T(8,128)(2,1)S(1)}, u32[]{:S(2)}, u32[]{:S(2)}) collective-permute-start(bf16[256,256]{1,0:T(8,128)(2,1)S(1)} %get-tuple-element.16), channel_id=1, source_target_pairs={{0,6},{1,7},{2,4},{3,5},{4,2},{5,3},{6,0},{7,1},{8,14},{9,15},{10,... | collective-permute-start | bytes 393224 | tf_op jit(solution)/shard_map/ppermute | solution.py:164
  39.3 6.8 %collective-permute-start.7 = (bf16[256,256]{1,0:T(8,128)(2,1)S(1)}, bf16[256,256]{1,0:T(8,128)(2,1)S(1)}, u32[]{:S(2)}, u32[]{:S(2)}) collective-permute-start(bf16[256,256]{1,0:T(8,128)(2,1)S(1)} %get-tuple-element.17), channel_id=1, source_target_pairs={{0,4},{1,5},{2,6},{3,7},{4,0},{5,1},{6,2},{7,3},{8,12},{9,13},{10,... | collective-permute-start | bytes 393224 | tf_op jit(solution)/shard_map/ppermute | solution.py:164
  39.3 6.8 %collective-permute-start.6 = (bf16[256,256]{1,0:T(8,128)(2,1)S(1)}, bf16[256,256]{1,0:T(8,128)(2,1)S(1)}, u32[]{:S(2)}, u32[]{:S(2)}) collective-permute-start(bf16[256,256]{1,0:T(8,128)(2,1)S(1)} %get-tuple-element.18), channel_id=1, source_target_pairs={{0,2},{1,3},{2,0},{3,1},{4,6},{5,7},{6,4},{7,5},{8,10},{9,11},{10,... | collective-permute-start | bytes 393224 | tf_op jit(solution)/shard_map/ppermute | solution.py:164
  46.1 19.4 %copy-start.7 = (f32[256,256]{1,0:T(8,128)S(1)}, f32[256,256]{1,0:T(8,128)}, u32[]{:S(2)}) copy-start(f32[256,256]{1,0:T(8,128)} %get-tuple-element.12) | copy-start | bytes 786436
  46.2 19.3 %collective-permute-start.9 = (bf16[256,256]{1,0:T(8,128)(2,1)S(1)}, bf16[256,256]{1,0:T(8,128)(2,1)S(1)}, u32[]{:S(2)}, u32[]{:S(2)}) collective-permute-start(bf16[256,256]{1,0:T(8,128)(2,1)S(1)} %fusion.7), channel_id=1, source_target_pairs={{8,0},{9,1},{10,2},{11,3},{12,4},{13,5},{14,6},{15,7},{16,8},{17,9... | collective-permute-start | bytes 393224 | tf_op jit(solution)/shard_map/ppermute | solution.py:217
